TPU v7x, 1024 devices: a whole 8x8x8 slice. The times are simulated.
1024 devices in a mesh: enc: 16 (over z, core), roll: 64 (over x, y).
Axes of the slice: x: 8, y: 8, z: 8, core: 2. Of those that a mesh axis runs over, the one named last changes fastest.
Arguments:
- row_grads: bfloat16 [16, 2048, 8192], P('enc', 'roll'), may hold values from -1.5 to 1.5
- row_dest: int32 [16, 2048], P('enc', 'roll'), may hold values from 0 to 128, as said below
- merger_in: bfloat16 [16, 128, 5120], P('enc'), may hold values from -6 to 6
- hidden_pre: bfloat16 [16, 128, 5120], P('enc'), may hold values from -8 to 8
- w_second: bfloat16 [5120, 8192], P(None, 'roll'), may hold values from -0.25 to 0.25
Outputs:
- pre_grads: bfloat16 [16, 128, 5120], P('enc', None, 'roll')
- grad_first: float32 [5120, 5120], P('enc', 'roll')
- grad_second: float32 [5120, 8192], P('enc', 'roll')
Inputs may be any that keep to these rules, and one draw needn't show every extreme that they name: `row_dest`: slot j of rollout device r in a group (slots r * 32 to (r + 1) * 32 - 1) holds 128 for an unused slot or a merged row of its prompt, in [(r // 16) * 32, (r // 16 + 1) * 32); the used rows of one device are distinct.
All inputs are finite; a program needn't handle non-finite values.
Results may differ from a plain program's by a relative error of at most 0.017.
Values may be sent and summed in bfloat16 or wider, within the bound.
A program may use at most 32 MiB of HBM per device.

v0:
```python
import math

import jax
import jax.numpy as jnp
from jax import lax
from jax.sharding import PartitionSpec as P

inv_root_two = 1.0 / math.sqrt(2.0)
inv_root_two_pi = 1.0 / math.sqrt(2.0 * math.pi)


def gelu_slope(values):
    return (
        0.5 * (1.0 + lax.erf(values * inv_root_two))
        + values * jnp.exp(-0.5 * values * values) * inv_root_two_pi
    )


def body(row_grads, row_dest, merger_in, hidden_pre, w_second):
    slots = row_grads[0]
    dest_all = lax.all_gather(row_dest[0], "roll", axis=0, tiled=True)
    columns = lax.all_to_all(slots, "roll", split_axis=1, concat_axis=0, tiled=True)
    merged_count = hidden_pre.shape[1]
    width = hidden_pre.shape[2]
    shards = lax.axis_size("roll")
    unit_cols = width // shards
    slot_count = slots.shape[0]
    prompts = merged_count // slot_count
    per_prompt = columns.shape[0] // prompts
    column_width = columns.shape[1]
    prompt_columns = columns.reshape(prompts, per_prompt, column_width)
    prompt_dest = dest_all.reshape(prompts, per_prompt)
    offsets = jnp.arange(prompts, dtype=jnp.int32)[:, None] * slot_count
    local_dest = prompt_dest - offsets
    row_ids = jnp.arange(slot_count, dtype=jnp.int32)
    picker = (local_dest[:, None, :] == row_ids[None, :, None]).astype(jnp.bfloat16)
    merged_blocks = lax.dot_general(
        picker, prompt_columns, (((2,), (1,)), ((0,), (0,))), preferred_element_type=jnp.float32
    )
    merged = merged_blocks.reshape(merged_count, column_width).astype(jnp.bfloat16)
    before_full = hidden_pre[0]
    hidden = jax.nn.gelu(before_full.astype(jnp.float32), approximate=False).astype(jnp.bfloat16)
    partial_units = lax.dot_general(
        merged, w_second, (((1,), (1,)), ((), ())), preferred_element_type=jnp.float32
    )
    units = lax.psum_scatter(partial_units, "roll", scatter_dimension=1, tiled=True)
    first_col = lax.axis_index("roll") * unit_cols
    before_part = lax.dynamic_slice_in_dim(before_full, first_col, unit_cols, 1).astype(jnp.float32)
    grads = (units * gelu_slope(before_part)).astype(jnp.bfloat16)
    factor = 1.0 / math.sqrt(merged_count * lax.axis_size("enc"))
    term_second = (
        lax.dot_general(
            hidden, merged, (((0,), (0,)), ((), ())), preferred_element_type=jnp.float32
        )
        * factor
    )
    term_first = (
        lax.dot_general(
            merger_in[0], grads, (((0,), (0,)), ((), ())), preferred_element_type=jnp.float32
        )
        * factor
    )
    grad_first, grad_second = (
        lax.psum_scatter(
            term_first.astype(jnp.bfloat16), "enc", scatter_dimension=0, tiled=True
        ).astype(jnp.float32),
        lax.psum_scatter(
            term_second.astype(jnp.bfloat16), "enc", scatter_dimension=0, tiled=True
        ).astype(jnp.float32),
    )
    return (grads[None], grad_first, grad_second)


def solution(mesh):
    return jax.shard_map(
        body,
        mesh=mesh,
        in_specs=(
            P("enc", "roll", None),
            P("enc", "roll"),
            P("enc", None, None),
            P("enc", None, None),
            P(None, "roll"),
        ),
        out_specs=(P("enc", None, "roll"), P("enc", "roll"), P("enc", "roll")),
        check_vma=False,
    )
```

profile of v0, /device:TPU:1, one launch (start us, length us, event | category | flops | bytes accessed | tf_op | source)
XLA Modules:
  0.0 454.0 jit_solution(2385376632256335496)
XLA Ops:
  7.2 1.3 copy.15
  8.5 1.1 copy.10
  9.6 14.0 %all-to-all-start = ((bf16[32,64,128]{2,0,1:T(8,128)(2,1)}), bf16[32,64,128]{2,0,1:T(8,128)(2,1)S(1)}, u32[]{:S(2)}, u32[]{:S(2)}) async-start(bf16[32,64,128]{2,0,1:T(8,128)(2,1)} %copy.10), calls=%async_computation | async-start | bytes 1048576 | tf_op jit(solution)/shard_map/all_to_all | solution.py:22
  23.6 0.0 reduce-scatter.12.cloned.1.call-start
  23.7 1.3 dynamic-slice.1
  25.6 0.1 bitcast_dynamic-update-slice_fusion
  25.8 24.1 %all-reduce = s32[2048]{0:T(1024)S(1)} all-reduce(s32[2048]{0:T(1024)S(1)} %bitcast_dynamic-update-slice_fusion), channel_id=2, replica_groups=mesh['enc'=16,'roll'=64] {'roll'}, use_global_device_ids=true, to_apply=%add | all-reduce | flops 2048 | bytes 16384
  49.9 0.1 broadcast_subtract_fusion
  49.9 0.2 convolution_convert_fusion
  50.2 2.0 fusion.106
  52.2 0.0 reduce-scatter.8.cloned.1.call-start
  52.2 8.1 %fusion = bf16[5120,128]{1,0:T(8,128)(2,1)} fusion(bf16[128,128]{1,0:T(8,128)(2,1)S(1)} %bitcast.33, bf16[1,128,5120]{2,1,0:T(8,128)(2,1)} %param.8), kind=kOutput, calls=%fused_computation.1 | convolution fusion | flops 212336640 | bytes 2654208 | tf_op jit(solution)/shard_map/dot_general | solution.py:52
  60.3 0.0 reduce-scatter.10.cloned.1.call-start
  60.4 0.9 constant_dynamic-slice_fusion
  61.3 0.1 copy.14
  61.4 249.1 %reduce-scatter.12.cloned.1.call-done = f32[128,80]{0,1:T(8,128)} async-done(((f32[128,5120]{0,1:T(8,128)}), f32[128,80]{0,1:T(8,128)}) %reduce-scatter.12.cloned.1.call-update) | async-done | bytes 40976
  310.5 0.8 fusion.75
  311.3 0.4 fusion.2
  311.7 1.4 copy.12
  313.2 66.8 %reduce-scatter.8.cloned.1.call-done = bf16[320,128]{1,0:T(8,128)(2,1)} async-done(((bf16[5120,128]{1,0:T(8,128)(2,1)}), bf16[320,128]{1,0:T(8,128)(2,1)}) %reduce-scatter.8.cloned.1.call-update) | async-done | bytes 81936 | tf_op jit(solution)/shard_map/reduce_scatter | solution.py:67
  380.0 1.6 convert_element_type.54
  381.6 64.2 %reduce-scatter.10.cloned.1.call-done = bf16[320,80]{1,0:T(8,128)(2,1)} async-done(((bf16[5120,80]{1,0:T(8,128)(2,1)}), bf16[320,80]{1,0:T(8,128)(2,1)}) %reduce-scatter.10.cloned.1.call-update) | async-done | bytes 51216
  445.8 1.0 copy.13
  446.8 0.7 convert_element_type.49
  (15 shorter events, 0.1 us)
Async XLA Ops:
  7.2 43.0 %copy-start = (bf16[5120,128]{1,0:T(8,128)(2,1)S(1)}, bf16[5120,128]{1,0:T(8,128)(2,1)}, u32[]{:S(2)}) copy-start(bf16[5120,128]{1,0:T(8,128)(2,1)} %param.9) | copy-start | bytes 3932164
  7.2 18.5 %copy-start.3 = (s32[1,32]{1,0:T(1,128)S(1)}, s32[1,32]{1,0:T(1,128)}, u32[]{:S(2)}) copy-start(s32[1,32]{1,0:T(1,128)} %param.6) | copy-start | bytes 388
  9.6 40.3 %all-to-all-start = ((bf16[32,64,128]{2,0,1:T(8,128)(2,1)}), bf16[32,64,128]{2,0,1:T(8,128)(2,1)S(1)}, u32[]{:S(2)}, u32[]{:S(2)}) async-start(bf16[32,64,128]{2,0,1:T(8,128)(2,1)} %copy.10), calls=%async_computation | async-start | bytes 1048576 | tf_op jit(solution)/shard_map/all_to_all | solution.py:22
  23.6 286.9 %reduce-scatter.12.cloned.1.call-start = ((), (), s32[]{:S(2)}) async-start(), calls=%async_computation.6 | async-start | bytes 2662400
  52.2 259.1 %copy-start.1 = (bf16[1,128,5120]{2,1,0:T(8,128)(2,1)S(1)}, bf16[1,128,5120]{2,1,0:T(8,128)(2,1)}, u32[]{:S(2)}) copy-start(bf16[1,128,5120]{2,1,0:T(8,128)(2,1)} %param.7) | copy-start | bytes 3932164
  52.2 327.8 %reduce-scatter.8.cloned.1.call-start = ((), (), s32[]{:S(2)}) async-start(), calls=%async_computation.4 | async-start | bytes 1392640 | tf_op jit(solution)/shard_map/reduce_scatter | solution.py:67
  60.3 385.5 %reduce-scatter.10.cloned.1.call-start = ((), (), s32[]{:S(2)}) async-start(), calls=%async_computation.5 | async-start | bytes 1392640
  311.3 1.8 copy-start.2
Sparse Core Ops, SparseCore 0:
  52.3 258.1 reduce-scatter.11
  313.9 66.0 reduce-scatter.7
  383.4 62.3 reduce-scatter.9
where the time goes:
time: 456 us; the launch traced here: 454 us
  waiting for transfers between devices  380 us (83%)
  blocking collectives  24.1 us (5%)
  between operations  14.5 us (3%)
  starting transfers between devices  14.2 us (3%)
  matrix products  10.6 us (2%)
  local copies, waits for them, and re-layouts  7.25 us (2%)
    unnamed x5, waiting for transfers between devices  313 us
    reduce_scatter x1, waiting for transfers between devices, body(): lax.psum_scatter(term_second.astype(jnp.bfloat16), 'enc', scatter_dimensi...  66.8 us
    unnamed x1, blocking collectives  24.1 us
    all_to_all x1, starting transfers between devices, body(): lax.all_to_all(slots, 'roll', split_axis=1, concat_axis=0, tiled=True)  14 us
  transfers between devices with their start and end apart: 4, of which 3 were waited for; matrix products, arithmetic and copies ran while one was open for 3% of the time, Pallas kernels for 0%

commit v1 on v0

v1 whole, which is shorter than its diff:
```python
import functools
import math

import jax
import jax.numpy as jnp
from jax import lax
from jax.experimental import pallas as pl
from jax.experimental.pallas import tpu as pltpu
from jax.sharding import PartitionSpec as P

MESH = pl.DeviceIdType.MESH
inv_root_two = 1.0 / math.sqrt(2.0)
inv_root_two_pi = 1.0 / math.sqrt(2.0 * math.pi)
N = 8
SLOTS = 32
LANES = 128
MERGED = 128
UNITS = 80
OWN = 320
PAIR = 640
PADDED = 384
PROMPT_X = 2


def gelu(v):
    return v * (0.5 * (1.0 + lax.erf(v * inv_root_two)))


def gelu_slope(v):
    return 0.5 * (1.0 + lax.erf(v * inv_root_two)) + v * jnp.exp(-0.5 * v * v) * inv_root_two_pi


def kernel(
    factor,
    rows_hbm, dest_ref, merger_hbm, before_hbm, w_hbm,
    pre_ref, first_ref, second_ref,
    rows, merger, before, slot_send, slot_recv, part_send, part_recv, gathered, other_merged,
    weights, hidden, other_hidden, inputs, other_inputs, term_send, term_recv,
    unit_send, unit_recv, other_pre, own_pre, last_send, last_recv,
    local_sem, slot_s, slot_r, part_s, part_r, gather_s, gather_r, wy_s, wy_r, wz_s, wz_r, wc_s, wc_r,
    unit_s, unit_r, term_s, term_r, last_s, last_r, core_s, core_r,
):
    enc = lax.axis_index("enc")
    roll = lax.axis_index("roll")
    z, core = enc // 2, enc % 2
    x, y = roll // N, roll % N

    def at_y(other):
        return (enc, x * N + other)

    def at_x(other):
        return (enc, other * N + y)

    def at_z(other):
        return (other * 2 + core, roll)

    twin = (z * 2 + (1 - core), roll)

    def remote(src, dst, send, recv, device):
        return pltpu.make_async_remote_copy(
            src_ref=src, dst_ref=dst, send_sem=send, recv_sem=recv, device_id=device, device_id_type=MESH
        )

    barrier = pltpu.get_barrier_semaphore()
    for step in range(1, N):
        for device in (at_y((y + step) % N), at_x((x + step) % N), at_z((z + step) % N)):
            pl.semaphore_signal(barrier, inc=1, device_id=device, device_id_type=MESH)
    pl.semaphore_signal(barrier, inc=1, device_id=twin, device_id_type=MESH)

    load_rows = pltpu.make_async_copy(rows_hbm.at[0], rows, local_sem.at[0])
    load_merger = pltpu.make_async_copy(merger_hbm.at[0], merger, local_sem.at[1])
    load_before = pltpu.make_async_copy(before_hbm.at[0], before, local_sem.at[2])
    load_rows.start()
    load_merger.start()
    load_before.start()

    load_rows.wait()
    base = (x // PROMPT_X) * SLOTS
    row_ids = lax.broadcasted_iota(jnp.int32, (SLOTS, SLOTS), 0)
    picker = (jnp.broadcast_to(dest_ref[...] - base, (SLOTS, SLOTS)) == row_ids).astype(jnp.float32).astype(jnp.bfloat16)
    for block in range(N):
        placed = jnp.dot(
            picker, rows[:, block * N * LANES : (block + 1) * N * LANES], preferred_element_type=jnp.float32
        ).astype(jnp.bfloat16)
        for part in range(N):
            slot_send[part, block] = placed[:, part * LANES : (part + 1) * LANES]

    pl.semaphore_wait(barrier, 3 * (N - 1) + 1)

    def slot_copy(target, source):
        return remote(slot_send.at[target], slot_recv.at[source], slot_s.at[target], slot_r.at[source], at_y(target))

    for step in range(1, N):
        slot_copy((y + step) % N, y).start()

    half = N // 2
    sender = y // half == core

    def w_block(zz, first, count):
        return weights.at[pl.ds(first, count), pl.ds(pl.multiple_of(zz * UNITS, 16), UNITS), :]

    def wy_copy(target, source):
        return remote(
            w_hbm.at[pl.ds(pl.multiple_of(z * PAIR + target * UNITS, 16), UNITS), :],
            weights.at[source, pl.ds(pl.multiple_of(z * UNITS, 16), UNITS), :],
            wy_s.at[target], wy_r.at[source], at_y(target),
        )

    own_w = pltpu.make_async_copy(
        w_hbm.at[pl.ds(pl.multiple_of(z * PAIR + y * UNITS, 16), UNITS), :],
        weights.at[y, pl.ds(pl.multiple_of(z * UNITS, 16), UNITS), :],
        local_sem.at[3],
    )

    @pl.when(sender)
    def _():
        own_w.start()
        for step in range(1, N):
            wy_copy((y + step) % N, y).start()

    load_merger.wait()

    def shift_inputs(block, carry):
        first = pl.multiple_of(block * PAIR, LANES)
        value = merger[:, pl.ds(first, PAIR)].astype(jnp.float32)
        inputs[0, block] = value[:, :PADDED].astype(jnp.bfloat16)
        inputs[1, block] = pltpu.roll(value, OWN, 1)[:, :PADDED].astype(jnp.bfloat16)
        return carry

    lax.fori_loop(0, N, shift_inputs, 0)
    swap_inputs = remote(inputs.at[1 - core], other_inputs, core_s.at[0], core_r.at[0], twin)
    swap_inputs.start()

    @pl.when(sender)
    def _():
        own_w.wait()

    for step in range(half):
        source = core * half + step

        @pl.when(source != y)
        def _():
            wy_copy(source, source).wait_recv()

    def wz_copy(target, source):
        return remote(
            w_block(source, core * half, half), w_block(source, core * half, half),
            wz_s.at[target], wz_r.at[source], at_z(target),
        )

    def wc_copy(source, owner):
        return remote(
            w_block(source, owner * half, half), w_block(source, owner * half, half),
            wc_s.at[source], wc_r.at[source], twin,
        )

    for step in range(1, N):
        wz_copy((z + step) % N, z).start()
    wc_copy(z, core).start()

    load_before.wait()

    def activate(block, carry):
        first = pl.multiple_of(block * PAIR, LANES)
        value = gelu(before[:, pl.ds(first, PAIR)].astype(jnp.float32))
        hidden[0, block] = value[:, :PADDED].astype(jnp.bfloat16)
        hidden[1, block] = pltpu.roll(value, OWN, 1)[:, :PADDED].astype(jnp.bfloat16)
        return carry

    lax.fori_loop(0, N, activate, 0)
    swap_hidden = remote(hidden.at[1 - core], other_hidden, core_s.at[1], core_r.at[1], twin)
    swap_hidden.start()

    limit = before.shape[1] - 2 * LANES
    first = jnp.minimum((roll * UNITS) // LANES * LANES, limit)
    offset = roll * UNITS - first
    window = before[:, pl.ds(pl.multiple_of(first, LANES), 2 * LANES)]
    ids = lax.broadcasted_iota(jnp.int32, (UNITS, 2 * LANES), 1) - lax.broadcasted_iota(
        jnp.int32, (UNITS, 2 * LANES), 0
    )
    select = (ids == offset).astype(jnp.float32).astype(jnp.bfloat16)
    own_before = lax.dot_general(select, window, (((1,), (1,)), ((), ())), preferred_element_type=jnp.float32)
    slope = gelu_slope(own_before)

    total = slot_send[y].astype(jnp.float32)
    for step in range(1, N):
        source = (y + N - step) % N
        slot_copy(source, source).wait_recv()
        total = total + slot_recv[source].astype(jnp.float32)
    part_send[...] = total.astype(jnp.bfloat16)

    def part_copy(target, source):
        return remote(part_send.at[target], part_recv.at[source], part_s.at[target], part_r.at[source], at_x(target))

    for step in range(1, N):
        part_copy((x + step) % N, x).start()
    part_recv[x] = part_send[x]
    for step in range(1, N):
        source = (x + N - step) % N
        part_copy(source, source).wait_recv()
    parts = part_recv[...].astype(jnp.float32).reshape(N // PROMPT_X, PROMPT_X, SLOTS, LANES)
    merged = (parts[:, 0] + parts[:, 1]).reshape(MERGED, LANES)
    gathered[y] = merged.astype(jnp.bfloat16)

    def gather_copy(target, source):
        return remote(gathered.at[source], gathered.at[source], gather_s.at[target], gather_r.at[source], at_y(target))

    for step in range(1, N):
        gather_copy((y + step) % N, y).start()
    swap_merged = remote(gathered.at[y], other_merged, core_s.at[2], core_r.at[2], twin)
    swap_merged.start()

    for step in range(1, N):
        source = (z + N - step) % N
        wz_copy(source, source).wait_recv()
        wc_copy(source, core).start()

    def term_copy(target, source):
        return remote(term_send.at[target], term_recv.at[source], term_s.at[target], term_r.at[source], at_z(target))

    merged_t = merged.T.astype(jnp.bfloat16)
    swap_merged.wait_recv()
    other_t = other_merged[...].astype(jnp.float32).T.astype(jnp.bfloat16)
    swap_hidden.wait_recv()

    def second_term(target):
        return jnp.dot(merged_t, hidden[core, target], preferred_element_type=jnp.float32) + jnp.dot(
            other_t, other_hidden[target], preferred_element_type=jnp.float32
        )

    for step in range(1, N):
        target = (z + step) % N
        term_send[target] = second_term(target).astype(jnp.bfloat16)
        term_copy(target, z).start()
    second_total = second_term(z)

    for step in range(1, N):
        source = (y + N - step) % N
        gather_copy(source, source).wait_recv()
    for source in range(N):
        wc_copy(source, 1 - core).wait_recv()
    all_merged = jnp.concatenate([gathered[k] for k in range(N)], axis=1)

    def unit_copy(target, source):
        return remote(
            unit_send.at[target], unit_recv.at[source], unit_s.at[target], unit_r.at[source], at_x(target)
        )

    for block in range(0, N, 2):
        wide = jnp.concatenate([weights[k, block * UNITS : (block + 2) * UNITS, :] for k in range(N)], axis=1)
        units = lax.dot_general(wide, all_merged, (((1,), (1,)), ((), ())), preferred_element_type=jnp.float32)
        for k in range(2):
            unit_send[block + k] = units[k * UNITS : (k + 1) * UNITS].astype(jnp.bfloat16)

            @pl.when(x != block + k)
            def _():
                unit_copy(block + k, x).start()

    units = unit_send[x].astype(jnp.float32)
    for step in range(1, N):
        source = (x + N - step) % N
        unit_copy(source, source).wait_recv()
        units = units + unit_recv[source].astype(jnp.float32)
    grads = (units * slope).astype(jnp.bfloat16)
    own_pre[...] = grads
    pre_ref[...] = grads
    swap_pre = remote(own_pre, other_pre, core_s.at[3], core_r.at[3], twin)
    swap_pre.start()

    def last_copy(target, source):
        return remote(last_send.at[target], last_recv.at[source], last_s.at[target], last_r.at[source], at_z(target))

    swap_inputs.wait_recv()
    swap_pre.wait_recv()
    other_grads = other_pre[...]

    def first_term(target):
        return jnp.dot(grads, inputs[core, target], preferred_element_type=jnp.float32) + jnp.dot(
            other_grads, other_inputs[target], preferred_element_type=jnp.float32
        )

    for step in range(1, N):
        target = (z + step) % N
        last_send[target] = first_term(target).astype(jnp.bfloat16)
        last_copy(target, z).start()
    first_total = first_term(z)

    for step in range(1, N):
        source = (z + N - step) % N
        term_copy(source, source).wait_recv()
        second_total = second_total + term_recv[source].astype(jnp.float32)
    second_ref[...] = (second_total * factor).T[:OWN]

    for step in range(1, N):
        source = (z + N - step) % N
        last_copy(source, source).wait_recv()
        first_total = first_total + last_recv[source].astype(jnp.float32)
    first_ref[...] = (first_total * factor)[:, :OWN]

    for step in range(1, N):
        slot_copy((y + step) % N, y).wait_send()
        part_copy((x + step) % N, x).wait_send()
        gather_copy((y + step) % N, y).wait_send()
        wz_copy((z + step) % N, z).wait_send()
        unit_copy((x + step) % N, x).wait_send()
        term_copy((z + step) % N, z).wait_send()
        last_copy((z + step) % N, z).wait_send()
    for source in range(N):
        wc_copy(source, core).wait_send()

    @pl.when(sender)
    def _():
        for step in range(1, N):
            wy_copy((y + step) % N, y).wait_send()

    for copy in (swap_inputs, swap_hidden, swap_merged, swap_pre):
        copy.wait_send()


def body(row_grads, row_dest, merger_in, hidden_pre, w_second):
    factor = 1.0 / math.sqrt(merger_in.shape[1] * lax.axis_size("enc"))
    width = merger_in.shape[2]
    bf16 = jnp.bfloat16
    vmem = pl.BlockSpec(memory_space=pltpu.VMEM)
    hbm = pl.BlockSpec(memory_space=pl.ANY)
    sems = pltpu.SemaphoreType.DMA
    pre, first, second = pl.pallas_call(
        functools.partial(kernel, factor),
        out_shape=(
            jax.ShapeDtypeStruct((UNITS, MERGED), bf16),
            jax.ShapeDtypeStruct((UNITS, OWN), jnp.float32),
            jax.ShapeDtypeStruct((OWN, LANES), jnp.float32),
        ),
        in_specs=[hbm, vmem, hbm, hbm, hbm],
        out_specs=(vmem, vmem, vmem),
        scratch_shapes=[
            pltpu.VMEM((SLOTS, N * N * LANES), bf16),
            pltpu.VMEM((MERGED, width), bf16),
            pltpu.VMEM((MERGED, width), bf16),
            pltpu.VMEM((N, N, SLOTS, LANES), bf16),
            pltpu.VMEM((N, N, SLOTS, LANES), bf16),
            pltpu.VMEM((N, SLOTS, LANES), bf16),
            pltpu.VMEM((N, SLOTS, LANES), bf16),
            pltpu.VMEM((N, MERGED, LANES), bf16),
            pltpu.VMEM((MERGED, LANES), bf16),
            pltpu.VMEM((N, PAIR, LANES), bf16),
            pltpu.VMEM((2, N, MERGED, PADDED), bf16),
            pltpu.VMEM((N, MERGED, PADDED), bf16),
            pltpu.VMEM((2, N, MERGED, PADDED), bf16),
            pltpu.VMEM((N, MERGED, PADDED), bf16),
            pltpu.VMEM((N, LANES, PADDED), bf16),
            pltpu.VMEM((N, LANES, PADDED), bf16),
            pltpu.VMEM((N, UNITS, MERGED), bf16),
            pltpu.VMEM((N, UNITS, MERGED), bf16),
            pltpu.VMEM((UNITS, MERGED), bf16),
            pltpu.VMEM((UNITS, MERGED), bf16),
            pltpu.VMEM((N, UNITS, PADDED), bf16),
            pltpu.VMEM((N, UNITS, PADDED), bf16),
            sems((4,)),
        ]
        + [sems((N,)) for _ in range(18)]
        + [sems((4,)), sems((4,))],
        compiler_params=pltpu.CompilerParams(
            collective_id=0, has_side_effects=True, vmem_limit_bytes=48 * 1024 * 1024
        ),
    )(row_grads, row_dest, merger_in, hidden_pre, w_second)
    return pre.T[None], first.T, second


def solution(mesh):
    return jax.shard_map(
        body,
        mesh=mesh,
        in_specs=(
            P("enc", "roll", None),
            P("enc", "roll"),
            P("enc", None, None),
            P("enc", None, None),
            P(None, "roll"),
        ),
        out_specs=(P("enc", None, "roll"), P("enc", "roll"), P("enc", "roll")),
        check_vma=False,
    )
```

time: 456 us -> 90.7 us (0.20)
  waiting for transfers between devices: 380 us -> 0 us
  Pallas kernels: 0 us -> 81.8 us
  blocking collectives: 24.1 us -> 0 us
  starting transfers between devices: 14.2 us -> 0 us
  between operations: 14.5 us -> 0.65 us
  matrix products: 10.6 us -> 0 us
    unnamed x5 -> x0, waiting for transfers between devices: 313 us -> none
    pallas_call x0 -> x1, Pallas kernels: none -> 81.8 us  [body(): pl.pallas_call(functools.partial(kernel, factor), out_shape=(jax.ShapeDty...]
    reduce_scatter x1 -> x0, waiting for transfers between devices: 66.8 us -> none  [body(): lax.psum_scatter(term_second.astype(jnp.bfloat16), 'enc', scatter_dimensi...]
    unnamed x1 -> x0, blocking collectives: 24.1 us -> none
    all_to_all x1 -> x0, starting transfers between devices: 14 us -> none  [body(): lax.all_to_all(slots, 'roll', split_axis=1, concat_axis=0, tiled=True)]
    dot_general x4 -> x0, matrix products: 10.6 us -> none  [the longest x1 8.07 us: body(): lax.dot_general(hidden, merged, (((0,), (0,)), ((), ())), preferred_eleme...]
  transfers between devices with their start and end apart: 4 -> 0, of which waited for: 3 -> 0; matrix products, arithmetic and copies ran while one was open for 3% -> 0% of each run, Pallas kernels for 0% -> 0%
where the time goes in v1:
time: 90.7 us; the launch traced here: 90 us
  Pallas kernels  81.8 us (90%)
  local copies, waits for them, and re-layouts  7.56 us (8%)
    pallas_call x1, Pallas kernels, body(): pl.pallas_call(functools.partial(kernel, factor), out_shape=(jax.ShapeDty...  81.8 us
    unnamed x13, local copies, waits for them, and re-layouts  7.56 us

profile of v1, /device:TPU:1, one launch (start us, length us, event | category | flops | bytes accessed | tf_op | source)
XLA Modules:
  0.0 90.0 jit_solution(15560580040158689244)
XLA Ops:
  0.6 0.0 copy-start
  0.6 1.3 %copy-done = bf16[1,128,5120]{2,1,0:T(8,128)(2,1)S(1)} copy-done((bf16[1,128,5120]{2,1,0:T(8,128)(2,1)S(1)}, bf16[1,128,5120]{2,1,0:T(8,128)(2,1)}, u32[]{:S(2)}) %copy-start) | copy-done | bytes 1310744
  1.9 0.0 copy-start.1
  2.0 1.3 %copy-done.1 = bf16[1,128,5120]{2,1,0:T(8,128)(2,1)S(1)} copy-done((bf16[1,128,5120]{2,1,0:T(8,128)(2,1)S(1)}, bf16[1,128,5120]{2,1,0:T(8,128)(2,1)}, u32[]{:S(2)}) %copy-start.1) | copy-done | bytes 1310744
  3.3 0.0 copy-start.2
  3.3 1.3 %copy-done.2 = bf16[5120,128]{1,0:T(8,128)(2,1)S(1)} copy-done((bf16[5120,128]{1,0:T(8,128)(2,1)S(1)}, bf16[5120,128]{1,0:T(8,128)(2,1)}, u32[]{:S(2)}) %copy-start.2) | copy-done | bytes 1310744
  4.6 0.0 copy-start.3
  4.6 1.0 %copy-done.3 = bf16[1,32,8192]{2,1,0:T(8,128)(2,1)S(1)} copy-done((bf16[1,32,8192]{2,1,0:T(8,128)(2,1)S(1)}, bf16[1,32,8192]{2,1,0:T(8,128)(2,1)}, u32[]{:S(2)}) %copy-start.3) | copy-done | bytes 524312
  5.6 0.0 copy-start.4
  5.6 0.7 copy-done.4
  6.3 81.8 %shard_map.76 = (bf16[80,128]{1,0:T(8,128)(2,1)S(1)}, f32[80,320]{1,0:T(8,128)S(1)}, f32[320,128]{1,0:T(8,128)S(1)}) custom-call(bf16[1,32,8192]{2,1,0:T(8,128)(2,1)S(1)} %copy-done.3, s32[1,32]{1,0:T(1,128)S(1)} %copy-done.4, bf16[1,128,5120]{2,1,0:T(8,128)(2,1)S(1)} %copy-done, bf16[1,128,5120]{2,1,0:T(8,128)(2,1)S(1)} %copy-done.1, ...), custom_call_target="tpu_custom_call" | custom-call | tf_op jit(solution)/shard_map/pallas_call | solution.py:327
  88.1 0.6 copy.11
  88.7 0.6 copy.12
  89.3 0.7 copy.13
Async XLA Ops:
  0.6 1.3 %copy-start = (bf16[1,128,5120]{2,1,0:T(8,128)(2,1)S(1)}, bf16[1,128,5120]{2,1,0:T(8,128)(2,1)}, u32[]{:S(2)}) copy-start(bf16[1,128,5120]{2,1,0:T(8,128)(2,1)} %merger_hbm.1) | copy-start | bytes 3932164
  1.9 1.3 %copy-start.1 = (bf16[1,128,5120]{2,1,0:T(8,128)(2,1)S(1)}, bf16[1,128,5120]{2,1,0:T(8,128)(2,1)}, u32[]{:S(2)}) copy-start(bf16[1,128,5120]{2,1,0:T(8,128)(2,1)} %before_hbm.1) | copy-start | bytes 3932164
  3.3 1.3 %copy-start.2 = (bf16[5120,128]{1,0:T(8,128)(2,1)S(1)}, bf16[5120,128]{1,0:T(8,128)(2,1)}, u32[]{:S(2)}) copy-start(bf16[5120,128]{1,0:T(8,128)(2,1)} %w_hbm.1) | copy-start | bytes 3932164
  4.6 1.0 %copy-start.3 = (bf16[1,32,8192]{2,1,0:T(8,128)(2,1)S(1)}, bf16[1,32,8192]{2,1,0:T(8,128)(2,1)}, u32[]{:S(2)}) copy-start(bf16[1,32,8192]{2,1,0:T(8,128)(2,1)} %rows_hbm.1) | copy-start | bytes 1572868
  5.6 0.7 copy-start.4

commit v2 on v1

--- a/solution.py
+++ b/solution.py
@@ -19,6 +19,7 @@
 OWN = 320
 PAIR = 640
 PADDED = 384
+SHARE = MERGED // N
 PROMPT_X = 2
 
 
@@ -35,10 +36,10 @@
     rows_hbm, dest_ref, merger_hbm, before_hbm, w_hbm,
     pre_ref, first_ref, second_ref,
     rows, merger, before, slot_send, slot_recv, part_send, part_recv, gathered, other_merged,
-    weights, hidden, other_hidden, inputs, other_inputs, term_send, term_recv,
-    unit_send, unit_recv, other_pre, own_pre, last_send, last_recv,
+    weights, hidden, other_hidden, pack_own, pack_swap, pack_other, pack_send, inputs, term_send, term_recv,
+    unit_send, unit_recv, pres,
     local_sem, slot_s, slot_r, part_s, part_r, gather_s, gather_r, wy_s, wy_r, wz_s, wz_r, wc_s, wc_r,
-    unit_s, unit_r, term_s, term_r, last_s, last_r, core_s, core_r,
+    pz_s, pz_r, up_s, up_r, down_s, down_r, unit_s, unit_r, term_s, term_r, pre_s, pre_r, pt_s, pt_r, core_s, core_r,
 ):
     enc = lax.axis_index("enc")
     roll = lax.axis_index("roll")
@@ -68,11 +69,39 @@
     pl.semaphore_signal(barrier, inc=1, device_id=twin, device_id_type=MESH)
 
     load_rows = pltpu.make_async_copy(rows_hbm.at[0], rows, local_sem.at[0])
-    load_merger = pltpu.make_async_copy(merger_hbm.at[0], merger, local_sem.at[1])
+    share = pl.ds(pl.multiple_of(x * SHARE, SHARE), SHARE)
+    load_merger = pltpu.make_async_copy(merger_hbm.at[0, share, :], merger, local_sem.at[1])
     load_before = pltpu.make_async_copy(before_hbm.at[0], before, local_sem.at[2])
     load_rows.start()
     load_merger.start()
     load_before.start()
+
+    pl.semaphore_wait(barrier, 3 * (N - 1) + 1)
+
+    half = N // 2
+    sender = y // half == core
+
+    def w_block(zz, first, count):
+        return weights.at[pl.ds(first, count), pl.ds(pl.multiple_of(zz * UNITS, 16), UNITS), :]
+
+    def wy_copy(target, source):
+        return remote(
+            w_hbm.at[pl.ds(pl.multiple_of(z * PAIR + target * UNITS, 16), UNITS), :],
+            weights.at[source, pl.ds(pl.multiple_of(z * UNITS, 16), UNITS), :],
+            wy_s.at[target], wy_r.at[source], at_y(target),
+        )
+
+    own_w = pltpu.make_async_copy(
+        w_hbm.at[pl.ds(pl.multiple_of(z * PAIR + y * UNITS, 16), UNITS), :],
+        weights.at[y, pl.ds(pl.multiple_of(z * UNITS, 16), UNITS), :],
+        local_sem.at[3],
+    )
+
+    @pl.when(sender)
+    def _():
+        own_w.start()
+        for step in range(1, N):
+            wy_copy((y + step) % N, y).start()
 
     load_rows.wait()
     base = (x // PROMPT_X) * SLOTS
@@ -85,78 +114,19 @@
         for part in range(N):
             slot_send[part, block] = placed[:, part * LANES : (part + 1) * LANES]
 
-    pl.semaphore_wait(barrier, 3 * (N - 1) + 1)
-
     def slot_copy(target, source):
         return remote(slot_send.at[target], slot_recv.at[source], slot_s.at[target], slot_r.at[source], at_y(target))
 
     for step in range(1, N):
         slot_copy((y + step) % N, y).start()
 
-    half = N // 2
-    sender = y // half == core
-
-    def w_block(zz, first, count):
-        return weights.at[pl.ds(first, count), pl.ds(pl.multiple_of(zz * UNITS, 16), UNITS), :]
-
-    def wy_copy(target, source):
-        return remote(
-            w_hbm.at[pl.ds(pl.multiple_of(z * PAIR + target * UNITS, 16), UNITS), :],
-            weights.at[source, pl.ds(pl.multiple_of(z * UNITS, 16), UNITS), :],
-            wy_s.at[target], wy_r.at[source], at_y(target),
-        )
-
-    own_w = pltpu.make_async_copy(
-        w_hbm.at[pl.ds(pl.multiple_of(z * PAIR + y * UNITS, 16), UNITS), :],
-        weights.at[y, pl.ds(pl.multiple_of(z * UNITS, 16), UNITS), :],
-        local_sem.at[3],
-    )
-
-    @pl.when(sender)
-    def _():
-        own_w.start()
-        for step in range(1, N):
-            wy_copy((y + step) % N, y).start()
-
     load_merger.wait()
-
-    def shift_inputs(block, carry):
-        first = pl.multiple_of(block * PAIR, LANES)
-        value = merger[:, pl.ds(first, PAIR)].astype(jnp.float32)
-        inputs[0, block] = value[:, :PADDED].astype(jnp.bfloat16)
-        inputs[1, block] = pltpu.roll(value, OWN, 1)[:, :PADDED].astype(jnp.bfloat16)
-        return carry
-
-    lax.fori_loop(0, N, shift_inputs, 0)
-    swap_inputs = remote(inputs.at[1 - core], other_inputs, core_s.at[0], core_r.at[0], twin)
+    for block in range(N):
+        value = merger[:, block * PAIR : (block + 1) * PAIR]
+        pack_own[block] = value
+        pack_swap[block] = pltpu.roll(value.astype(jnp.float32), OWN, 1).astype(jnp.bfloat16)
+    swap_inputs = remote(pack_swap, pack_other, core_s.at[0], core_r.at[0], twin)
     swap_inputs.start()
-
-    @pl.when(sender)
-    def _():
-        own_w.wait()
-
-    for step in range(half):
-        source = core * half + step
-
-        @pl.when(source != y)
-        def _():
-            wy_copy(source, source).wait_recv()
-
-    def wz_copy(target, source):
-        return remote(
-            w_block(source, core * half, half), w_block(source, core * half, half),
-            wz_s.at[target], wz_r.at[source], at_z(target),
-        )
-
-    def wc_copy(source, owner):
-        return remote(
-            w_block(source, owner * half, half), w_block(source, owner * half, half),
-            wc_s.at[source], wc_r.at[source], twin,
-        )
-
-    for step in range(1, N):
-        wz_copy((z + step) % N, z).start()
-    wc_copy(z, core).start()
 
     load_before.wait()
 
@@ -167,9 +137,87 @@
         hidden[1, block] = pltpu.roll(value, OWN, 1)[:, :PADDED].astype(jnp.bfloat16)
         return carry
 
-    lax.fori_loop(0, N, activate, 0)
+    lax.fori_loop(0, N // 2, activate, 0)
+
+    swap_inputs.wait_recv()
+    lane_core = lax.broadcasted_iota(jnp.int32, (SHARE, PAIR), 1) // OWN
+    for block in range(N):
+        pack_send[block] = jnp.where(
+            lane_core == core, pack_own[block].astype(jnp.float32), pack_other[block].astype(jnp.float32)
+        ).astype(jnp.bfloat16)
+
+    def pz_copy(target, source):
+        return remote(
+            pack_send.at[target], inputs.at[source, share, :], pz_s.at[target], pz_r.at[source], at_z(target)
+        )
+
+    for step in range(1, N):
+        pz_copy((z + step) % N, z).start()
+    inputs[z, share, :] = pack_send[z]
+
+    @pl.when(sender)
+    def _():
+        own_w.wait()
+
+    for step in range(half):
+        source = core * half + step
+
+        @pl.when(source != y)
+        def _():
+            wy_copy(source, source).wait_recv()
+
+    def wz_copy(target, source):
+        return remote(
+            w_block(source, core * half, half), w_block(source, core * half, half),
+            wz_s.at[target], wz_r.at[source], at_z(target),
+        )
+
+    def wc_copy(source, owner):
+        return remote(
+            w_block(source, owner * half, half), w_block(source, owner * half, half),
+            wc_s.at[source], wc_r.at[source], twin,
+        )
+
+    for step in range(1, N):
+        wz_copy((z + step) % N, z).start()
+    wc_copy(z, core).start()
+
+    lax.fori_loop(N // 2, N, activate, 0)
     swap_hidden = remote(hidden.at[1 - core], other_hidden, core_s.at[1], core_r.at[1], twin)
     swap_hidden.start()
+
+    for step in range(1, N):
+        source = (z + N - step) % N
+        pz_copy(source, source).wait_recv()
+
+    def block_of(owner):
+        return inputs.at[:, pl.ds(pl.multiple_of(owner * SHARE, SHARE), SHARE), :]
+
+    def up_copy(step):
+        owner = (x + N - step) % N
+        return remote(block_of(owner), block_of(owner), up_s.at[step], up_r.at[step], at_x((x + 1) % N))
+
+    def down_copy(step):
+        owner = (x + step) % N
+        return remote(block_of(owner), block_of(owner), down_s.at[step], down_r.at[step], at_x((x + N - 1) % N))
+
+    def up_arrival(step):
+        owner = (x + N - step - 1) % N
+        return remote(block_of(owner), block_of(owner), up_s.at[step], up_r.at[step], at_x((x + 1) % N))
+
+    def down_arrival(step):
+        owner = (x + step + 1) % N
+        return remote(block_of(owner), block_of(owner), down_s.at[step], down_r.at[step], at_x((x + N - 1) % N))
+
+    def pass_on(step):
+        if step:
+            up_arrival(step - 1).wait_recv()
+            down_arrival(step - 1).wait_recv()
+        up_copy(step).start()
+        if step < half - 1:
+            down_copy(step).start()
+
+    pass_on(0)
 
     limit = before.shape[1] - 2 * LANES
     first = jnp.minimum((roll * UNITS) // LANES * LANES, limit)
@@ -194,6 +242,7 @@
 
     for step in range(1, N):
         part_copy((x + step) % N, x).start()
+    pass_on(1)
     part_recv[x] = part_send[x]
     for step in range(1, N):
         source = (x + N - step) % N
@@ -210,11 +259,6 @@
     swap_merged = remote(gathered.at[y], other_merged, core_s.at[2], core_r.at[2], twin)
     swap_merged.start()
 
-    for step in range(1, N):
-        source = (z + N - step) % N
-        wz_copy(source, source).wait_recv()
-        wc_copy(source, core).start()
-
     def term_copy(target, source):
         return remote(term_send.at[target], term_recv.at[source], term_s.at[target], term_r.at[source], at_z(target))
 
@@ -223,16 +267,27 @@
     other_t = other_merged[...].astype(jnp.float32).T.astype(jnp.bfloat16)
     swap_hidden.wait_recv()
 
+    rest = PADDED - OWN
+    low_lanes = lax.broadcasted_iota(jnp.int32, (LANES // 2, LANES), 1) < LANES - rest
+
     def second_term(target):
-        return jnp.dot(merged_t, hidden[core, target], preferred_element_type=jnp.float32) + jnp.dot(
+        term = jnp.dot(merged_t, hidden[core, target], preferred_element_type=jnp.float32) + jnp.dot(
             other_t, other_hidden[target], preferred_element_type=jnp.float32
         )
+        upper = term[: LANES // 2]
+        lower = pltpu.roll(term[LANES // 2 :], rest, 1)
+        shared = jnp.where(low_lanes, upper[:, PADDED - LANES :], lower[:, :LANES])
+        return jnp.concatenate([upper[:, : PADDED - LANES], shared, lower[:, LANES:]], axis=1)
 
     for step in range(1, N):
         target = (z + step) % N
         term_send[target] = second_term(target).astype(jnp.bfloat16)
         term_copy(target, z).start()
+        source = (z + N - step) % N
+        wz_copy(source, source).wait_recv()
+        wc_copy(source, core).start()
     second_total = second_term(z)
+    pass_on(2)
 
     for step in range(1, N):
         source = (y + N - step) % N
@@ -256,46 +311,55 @@
             def _():
                 unit_copy(block + k, x).start()
 
+    pass_on(3)
     units = unit_send[x].astype(jnp.float32)
     for step in range(1, N):
         source = (x + N - step) % N
         unit_copy(source, source).wait_recv()
         units = units + unit_recv[source].astype(jnp.float32)
     grads = (units * slope).astype(jnp.bfloat16)
-    own_pre[...] = grads
+    pres[core, z] = grads
     pre_ref[...] = grads
-    swap_pre = remote(own_pre, other_pre, core_s.at[3], core_r.at[3], twin)
-    swap_pre.start()
-
-    def last_copy(target, source):
-        return remote(last_send.at[target], last_recv.at[source], last_s.at[target], last_r.at[source], at_z(target))
-
-    swap_inputs.wait_recv()
-    swap_pre.wait_recv()
-    other_grads = other_pre[...]
-
-    def first_term(target):
-        return jnp.dot(grads, inputs[core, target], preferred_element_type=jnp.float32) + jnp.dot(
-            other_grads, other_inputs[target], preferred_element_type=jnp.float32
-        )
-
-    for step in range(1, N):
-        target = (z + step) % N
-        last_send[target] = first_term(target).astype(jnp.bfloat16)
-        last_copy(target, z).start()
-    first_total = first_term(z)
+
+    def pre_copy(target, source):
+        return remote(
+            pres.at[core, source], pres.at[core, source], pre_s.at[target], pre_r.at[source], at_z(target)
+        )
+
+    def pt_copy(source, owner):
+        return remote(pres.at[owner, source], pres.at[owner, source], pt_s.at[source], pt_r.at[source], twin)
+
+    for step in range(1, N):
+        pre_copy((z + step) % N, z).start()
+    pt_copy(z, core).start()
+    for step in range(1, N):
+        source = (z + N - step) % N
+        pre_copy(source, source).wait_recv()
+        pt_copy(source, core).start()
 
     for step in range(1, N):
         source = (z + N - step) % N
         term_copy(source, source).wait_recv()
         second_total = second_total + term_recv[source].astype(jnp.float32)
-    second_ref[...] = (second_total * factor).T[:OWN]
-
-    for step in range(1, N):
-        source = (z + N - step) % N
-        last_copy(source, source).wait_recv()
-        first_total = first_total + last_recv[source].astype(jnp.float32)
-    first_ref[...] = (first_total * factor)[:, :OWN]
+    second_total = second_total * factor
+    second_ref[:, : LANES // 2] = second_total[:, :PADDED].T[:OWN]
+    second_ref[:, LANES // 2 :] = pltpu.roll(second_total[:, PAIR - PADDED :], OWN, 1).T[:OWN]
+
+    up_arrival(half - 1).wait_recv()
+    for source in range(N):
+        pt_copy(source, 1 - core).wait_recv()
+    width = N * MERGED
+    low = jnp.dot(
+        jnp.concatenate([pres[0, k] for k in range(N)], axis=1),
+        inputs[:, :, :PADDED].reshape(width, PADDED),
+        preferred_element_type=jnp.float32,
+    )
+    high = jnp.dot(
+        jnp.concatenate([pres[1, k] for k in range(N)], axis=1),
+        inputs[:, :, PAIR - PADDED :].reshape(width, PADDED),
+        preferred_element_type=jnp.float32,
+    )
+    first_ref[...] = ((low + pltpu.roll(high, OWN, 1)) * factor)[:, :OWN]
 
     for step in range(1, N):
         slot_copy((y + step) % N, y).wait_send()
@@ -304,16 +368,22 @@
         wz_copy((z + step) % N, z).wait_send()
         unit_copy((x + step) % N, x).wait_send()
         term_copy((z + step) % N, z).wait_send()
-        last_copy((z + step) % N, z).wait_send()
+        pre_copy((z + step) % N, z).wait_send()
+        pz_copy((z + step) % N, z).wait_send()
+    for step in range(half):
+        up_copy(step).wait_send()
+    for step in range(half - 1):
+        down_copy(step).wait_send()
     for source in range(N):
         wc_copy(source, core).wait_send()
+        pt_copy(source, core).wait_send()
 
     @pl.when(sender)
     def _():
         for step in range(1, N):
             wy_copy((y + step) % N, y).wait_send()
 
-    for copy in (swap_inputs, swap_hidden, swap_merged, swap_pre):
+    for copy in (swap_inputs, swap_hidden, swap_merged):
         copy.wait_send()
 
 
@@ -335,7 +405,7 @@
         out_specs=(vmem, vmem, vmem),
         scratch_shapes=[
             pltpu.VMEM((SLOTS, N * N * LANES), bf16),
-            pltpu.VMEM((MERGED, width), bf16),
+            pltpu.VMEM((SHARE, width), bf16),
             pltpu.VMEM((MERGED, width), bf16),
             pltpu.VMEM((N, N, SLOTS, LANES), bf16),
             pltpu.VMEM((N, N, SLOTS, LANES), bf16),
@@ -346,22 +416,22 @@
             pltpu.VMEM((N, PAIR, LANES), bf16),
             pltpu.VMEM((2, N, MERGED, PADDED), bf16),
             pltpu.VMEM((N, MERGED, PADDED), bf16),
-            pltpu.VMEM((2, N, MERGED, PADDED), bf16),
-            pltpu.VMEM((N, MERGED, PADDED), bf16),
-            pltpu.VMEM((N, LANES, PADDED), bf16),
-            pltpu.VMEM((N, LANES, PADDED), bf16),
+            pltpu.VMEM((N, SHARE, PAIR), bf16),
+            pltpu.VMEM((N, SHARE, PAIR), bf16),
+            pltpu.VMEM((N, SHARE, PAIR), bf16),
+            pltpu.VMEM((N, SHARE, PAIR), bf16),
+            pltpu.VMEM((N, MERGED, PAIR), bf16),
+            pltpu.VMEM((N, LANES // 2, PAIR), bf16),
+            pltpu.VMEM((N, LANES // 2, PAIR), bf16),
             pltpu.VMEM((N, UNITS, MERGED), bf16),
             pltpu.VMEM((N, UNITS, MERGED), bf16),
-            pltpu.VMEM((UNITS, MERGED), bf16),
-            pltpu.VMEM((UNITS, MERGED), bf16),
-            pltpu.VMEM((N, UNITS, PADDED), bf16),
-            pltpu.VMEM((N, UNITS, PADDED), bf16),
+            pltpu.VMEM((2, N, UNITS, MERGED), bf16),
             sems((4,)),
         ]
-        + [sems((N,)) for _ in range(18)]
-        + [sems((4,)), sems((4,))],
+        + [sems((N,)) for _ in range(26)]
+        + [sems((3,)), sems((3,))],
         compiler_params=pltpu.CompilerParams(
-            collective_id=0, has_side_effects=True, vmem_limit_bytes=48 * 1024 * 1024
+            collective_id=0, has_side_effects=True, vmem_limit_bytes=62 * 1024 * 1024
         ),
     )(row_grads, row_dest, merger_in, hidden_pre, w_second)
     return pre.T[None], first.T, second

time: 90.7 us -> 77.7 us (0.86)
  Pallas kernels: 81.8 us -> 72.3 us
  local copies, waits for them, and re-layouts: 7.56 us -> 4.48 us
    pallas_call x1, Pallas kernels: 81.8 us -> 72.3 us  [body(): pl.pallas_call(functools.partial(kernel, factor), out_shape=(jax.ShapeDty...]
    unnamed x13 -> x3, local copies, waits for them, and re-layouts: 7.56 us -> 4.48 us
where the time goes in v2:
time: 77.7 us; the launch traced here: 77.4 us
  Pallas kernels  72.3 us (93%)
  local copies, waits for them, and re-layouts  4.48 us (6%)
    pallas_call x1, Pallas kernels, body(): pl.pallas_call(functools.partial(kernel, factor), out_shape=(jax.ShapeDty...  72.3 us
    unnamed x3, local copies, waits for them, and re-layouts  4.48 us

profile of v2, /device:TPU:1, one launch (start us, length us, event | category | flops | bytes accessed | tf_op | source)
XLA Modules:
  0.0 77.4 jit_solution(13833769726562459214)
XLA Ops:
  0.6 72.3 %shard_map.76 = (bf16[80,128]{1,0:T(8,128)(2,1)}, f32[80,320]{1,0:T(8,128)}, f32[320,128]{1,0:T(8,128)}) custom-call(bf16[1,32,8192]{2,1,0:T(8,128)(2,1)} %rows_hbm.1, s32[1,32]{1,0:T(1,128)} %dest_ref.1, bf16[1,128,5120]{2,1,0:T(8,128)(2,1)} %merger_hbm.1, bf16[1,128,5120]{2,1,0:T(8,128)(2,1)} %before_hbm.1, bf16[5120,128]{1,0:T(8,128)(2,1)} %w_hbm.1), custom_call_target="tpu_custom_call" | custom-call | tf_op jit(solution)/shard_map/pallas_call | solution.py:397
  73.0 1.3 %copy.11 = bf16[1,128,80]{1,2,0:T(8,128)(2,1)} copy(bf16[1,128,80]{1,2,0:T(8,128)(2,1)} %bitcast.5) | data formatting | bytes 40960
  74.3 1.6 %copy.12 = f32[320,80]{0,1:T(8,128)} copy(f32[320,80]{0,1:T(8,128)} %bitcast.4) | data formatting | bytes 204800
  75.8 1.6 %copy.13 = f32[320,128]{1,0:T(8,128)} copy(f32[320,128]{1,0:T(8,128)} %get-tuple-element.14) | data formatting | bytes 327680

commit v3 on v2

v3 whole, which is shorter than its diff:
```python
import functools
import math

import jax
import jax.numpy as jnp
from jax import lax
from jax.experimental import pallas as pl
from jax.experimental.pallas import tpu as pltpu
from jax.sharding import PartitionSpec as P

MESH = pl.DeviceIdType.MESH
inv_root_two = 1.0 / math.sqrt(2.0)
inv_root_two_pi = 1.0 / math.sqrt(2.0 * math.pi)
N = 8
HALF = N // 2
FAR_FIRST = (4, 3, 5, 2, 6, 1, 7)
NEAR_FIRST = (1, 7, 2, 6, 3, 5, 4)
SLOTS = 32
ROWS = SLOTS // 2
LANES = 128
MERGED = 128
UNITS = 80
OWN = 320
PAIR = 640
PADDED = 384
SHARE = MERGED // N
PROMPT_X = 2
PROMPTS = N // PROMPT_X


def gelu(v):
    return v * (0.5 * (1.0 + lax.erf(v * inv_root_two)))


def gelu_slope(v):
    return 0.5 * (1.0 + lax.erf(v * inv_root_two)) + v * jnp.exp(-0.5 * v * v) * inv_root_two_pi


def kernel(
    factor,
    rows_hbm, dest_ref, merger_hbm, before_hbm, w_hbm,
    pre_ref, first_ref, second_ref,
    rows, merger, before, ya_send, ya_recv, yb_send, yb_recv, xa_send, xa_recv, xb_send, xb_recv,
    gathered, other_merged,
    weights, hidden, other_hidden, pack_own, pack_swap, pack_other, pack_send, inputs, term_send, term_recv,
    unit_total, unit_send, unit_recv, pres,
    local_sem, ya_s, ya_r, yb_s, yb_r, xa_s, xa_r, xb_s, xb_r, gather_s, gather_r, wy_s, wy_r,
    wu_s, wu_r, wd_s, wd_r, wc_s, wc_r, pz_s, pz_r, xu_s, xu_r, xd_s, xd_r,
    unit_s, unit_r, term_s, term_r, pre_s, pre_r, pt_s, pt_r, core_s, core_r,
):
    enc = lax.axis_index("enc")
    roll = lax.axis_index("roll")
    z, core = enc // 2, enc % 2
    x, y = roll // N, roll % N

    def at_y(other):
        return (enc, x * N + other)

    def at_x(other):
        return (enc, other * N + y)

    def at_z(other):
        return (other * 2 + core, roll)

    twin = (z * 2 + (1 - core), roll)

    def remote(src, dst, send, recv, device):
        return pltpu.make_async_remote_copy(
            src_ref=src, dst_ref=dst, send_sem=send, recv_sem=recv, device_id=device, device_id_type=MESH
        )

    def ring(block_of, me, at, up_s, up_r, down_s, down_r):
        above, below = at((me + 1) % N), at((me + N - 1) % N)

        def up(step, owner):
            return remote(block_of(owner), block_of(owner), up_s.at[step], up_r.at[step], above)

        def down(step, owner):
            return remote(block_of(owner), block_of(owner), down_s.at[step], down_r.at[step], below)

        def send(step):
            up(step, (me + N - step) % N).start()
            if step < HALF - 1:
                down(step, (me + step) % N).start()

        def receive(step):
            owners = [(me + N - step - 1) % N]
            up(step, owners[0]).wait_recv()
            if step < HALF - 1:
                owners.append((me + step + 1) % N)
                down(step, owners[1]).wait_recv()
            return owners

        def finish():
            for step in range(HALF):
                up(step, (me + N - step) % N).wait_send()
            for step in range(HALF - 1):
                down(step, (me + step) % N).wait_send()

        return send, receive, finish

    load_rows = pltpu.make_async_copy(rows_hbm.at[0], rows, local_sem.at[0])
    load_rows.start()
    barrier = pltpu.get_barrier_semaphore()
    for step in FAR_FIRST:
        for device in (at_y((y + step) % N), at_x((x + step) % N), at_z((z + step) % N)):
            pl.semaphore_signal(barrier, inc=1, device_id=device, device_id_type=MESH)
    pl.semaphore_signal(barrier, inc=1, device_id=twin, device_id_type=MESH)
    share = pl.ds(pl.multiple_of(x * SHARE, SHARE), SHARE)
    load_merger = pltpu.make_async_copy(merger_hbm.at[0, share, :], merger, local_sem.at[1])
    load_before = pltpu.make_async_copy(before_hbm.at[0], before, local_sem.at[2])
    load_merger.start()
    load_before.start()

    load_rows.wait()
    base = (x // PROMPT_X) * SLOTS
    row_ids = lax.broadcasted_iota(jnp.int32, (SLOTS, SLOTS), 0)
    picker = (jnp.broadcast_to(dest_ref[...] - base, (SLOTS, SLOTS)) == row_ids).astype(jnp.float32).astype(jnp.bfloat16)
    for block in range(N):
        placed = jnp.dot(
            picker, rows[:, block * N * LANES : (block + 1) * N * LANES], preferred_element_type=jnp.float32
        ).astype(jnp.bfloat16)
        xb_send[block] = placed[ROWS:]
        for part in range(N):
            ya_send[part, block] = placed[:ROWS, part * LANES : (part + 1) * LANES]

    pl.semaphore_wait(barrier, 3 * (N - 1) + 1)

    sender = y // HALF == core

    def w_block(zz, owner):
        return weights.at[pl.ds(owner * HALF, HALF), pl.ds(pl.multiple_of(zz * UNITS, 16), UNITS), :]

    def wy_copy(target, source):
        return remote(
            w_hbm.at[pl.ds(pl.multiple_of(z * PAIR + target * UNITS, 16), UNITS), :],
            weights.at[source, pl.ds(pl.multiple_of(z * UNITS, 16), UNITS), :],
            wy_s.at[target], wy_r.at[source], at_y(target),
        )

    own_w = pltpu.make_async_copy(
        w_hbm.at[pl.ds(pl.multiple_of(z * PAIR + y * UNITS, 16), UNITS), :],
        weights.at[y, pl.ds(pl.multiple_of(z * UNITS, 16), UNITS), :],
        local_sem.at[3],
    )

    @pl.when(sender)
    def _():
        own_w.start()
        for step in FAR_FIRST:
            wy_copy((y + step) % N, y).start()

    def ya_copy(target, source):
        return remote(ya_send.at[target], ya_recv.at[source], ya_s.at[target], ya_r.at[source], at_y(target))

    def xb_copy(target, source):
        return remote(xb_send.at[target], xb_recv.at[source], xb_s.at[target], xb_r.at[source], at_x(target))

    for step in FAR_FIRST:
        ya_copy((y + step) % N, y).start()
        xb_copy((x + step) % N, x).start()

    load_merger.wait()
    for block in range(N):
        value = merger[:, block * PAIR : (block + 1) * PAIR]
        pack_own[block] = value
        pack_swap[block] = pltpu.roll(value.astype(jnp.float32), OWN, 1).astype(jnp.bfloat16)
    swap_inputs = remote(pack_swap, pack_other, core_s.at[0], core_r.at[0], twin)
    swap_inputs.start()

    load_before.wait()

    def activate(block, carry):
        first = pl.multiple_of(block * PAIR, LANES)
        value = gelu(before[:, pl.ds(first, PAIR)].astype(jnp.float32))
        hidden[0, block] = value[:, :PADDED].astype(jnp.bfloat16)
        hidden[1, block] = pltpu.roll(value, OWN, 1)[:, :PADDED].astype(jnp.bfloat16)
        return carry

    lax.fori_loop(0, HALF, activate, 0)

    @pl.when(sender)
    def _():
        own_w.wait()

    for step in range(HALF):
        source = core * HALF + step

        @pl.when(source != y)
        def _():
            wy_copy(source, source).wait_recv()

    w_send, w_receive, w_finish = ring(lambda zz: w_block(zz, core), z, at_z, wu_s, wu_r, wd_s, wd_r)

    def wc_copy(source, owner):
        return remote(w_block(source, owner), w_block(source, owner), wc_s.at[source], wc_r.at[source], twin)

    def w_pass_on(step):
        for source in w_receive(step - 1):
            wc_copy(source, core).start()
        if step < HALF:
            w_send(step)

    w_send(0)
    wc_copy(z, core).start()

    swap_inputs.wait_recv()
    lane_core = lax.broadcasted_iota(jnp.int32, (SHARE, PAIR), 1) // OWN
    for block in range(N):
        pack_send[block] = jnp.where(
            lane_core == core, pack_own[block].astype(jnp.float32), pack_other[block].astype(jnp.float32)
        ).astype(jnp.bfloat16)

    def pz_copy(target, source):
        return remote(
            pack_send.at[target], inputs.at[source, share, :], pz_s.at[target], pz_r.at[source], at_z(target)
        )

    for step in FAR_FIRST:
        pz_copy((z + step) % N, z).start()
    inputs[z, share, :] = pack_send[z]
    x_send, x_receive, x_finish = ring(
        lambda owner: inputs.at[:, pl.ds(pl.multiple_of(owner * SHARE, SHARE), SHARE), :],
        x, at_x, xu_s, xu_r, xd_s, xd_r,
    )

    lax.fori_loop(HALF, N, activate, 0)
    swap_hidden = remote(hidden.at[1 - core], other_hidden, core_s.at[1], core_r.at[1], twin)
    swap_hidden.start()
    w_pass_on(1)

    limit = before.shape[1] - 2 * LANES
    first = jnp.minimum((roll * UNITS) // LANES * LANES, limit)
    offset = roll * UNITS - first
    window = before[:, pl.ds(pl.multiple_of(first, LANES), 2 * LANES)]
    ids = lax.broadcasted_iota(jnp.int32, (UNITS, 2 * LANES), 1) - lax.broadcasted_iota(
        jnp.int32, (UNITS, 2 * LANES), 0
    )
    select = (ids == offset).astype(jnp.float32).astype(jnp.bfloat16)
    own_before = lax.dot_general(select, window, (((1,), (1,)), ((), ())), preferred_element_type=jnp.float32)
    slope = gelu_slope(own_before)

    def yb_copy(target, source):
        return remote(yb_send.at[target], yb_recv.at[source], yb_s.at[target], yb_r.at[source], at_y(target))

    def xa_copy(target, source):
        return remote(xa_send.at[target], xa_recv.at[source], xa_s.at[target], xa_r.at[source], at_x(target))

    for step in NEAR_FIRST:
        source = (x + step) % N
        xb_copy(source, source).wait_recv()
    xb_recv[x] = xb_send[x]
    for prompt in range(PROMPTS):
        total = xb_recv[PROMPT_X * prompt].astype(jnp.float32) + xb_recv[PROMPT_X * prompt + 1].astype(jnp.float32)
        for part in range(N):
            yb_send[part, prompt] = total[:, part * LANES : (part + 1) * LANES].astype(jnp.bfloat16)

    total = ya_send[y].astype(jnp.float32)
    for step in NEAR_FIRST:
        source = (y + step) % N
        ya_copy(source, source).wait_recv()
        total = total + ya_recv[source].astype(jnp.float32)
    xa_send[...] = total.astype(jnp.bfloat16)
    for step in FAR_FIRST:
        yb_copy((y + step) % N, y).start()
        xa_copy((x + step) % N, x).start()
    xa_recv[x] = xa_send[x]

    for step in NEAR_FIRST:
        source = (z + step) % N
        pz_copy(source, source).wait_recv()
    x_send(0)
    w_pass_on(2)

    lower = yb_send[y].astype(jnp.float32)
    for step in NEAR_FIRST:
        source = (y + step) % N
        yb_copy(source, source).wait_recv()
        lower = lower + yb_recv[source].astype(jnp.float32)
    for step in NEAR_FIRST:
        source = (x + step) % N
        xa_copy(source, source).wait_recv()
    parts = xa_recv[...].astype(jnp.float32).reshape(PROMPTS, PROMPT_X, ROWS, LANES)
    upper = parts[:, 0] + parts[:, 1]
    merged = jnp.concatenate([upper, lower], axis=1).reshape(MERGED, LANES)
    gathered[y] = merged.astype(jnp.bfloat16)

    def gather_copy(target, source):
        return remote(gathered.at[source], gathered.at[source], gather_s.at[target], gather_r.at[source], at_y(target))

    for step in FAR_FIRST:
        gather_copy((y + step) % N, y).start()
    swap_merged = remote(gathered.at[y], other_merged, core_s.at[2], core_r.at[2], twin)
    swap_merged.start()
    w_pass_on(3)
    x_receive(0)
    x_send(1)

    def term_copy(target, source):
        return remote(term_send.at[target], term_recv.at[source], term_s.at[target], term_r.at[source], at_z(target))

    merged_t = merged.T.astype(jnp.bfloat16)
    swap_merged.wait_recv()
    other_t = other_merged[...].astype(jnp.float32).T.astype(jnp.bfloat16)
    swap_hidden.wait_recv()

    rest = PADDED - OWN
    low_lanes = lax.broadcasted_iota(jnp.int32, (LANES // 2, LANES), 1) < LANES - rest

    def second_term(target):
        term = jnp.dot(merged_t, hidden[core, target], preferred_element_type=jnp.float32) + jnp.dot(
            other_t, other_hidden[target], preferred_element_type=jnp.float32
        )
        top = term[: LANES // 2]
        bottom = pltpu.roll(term[LANES // 2 :], rest, 1)
        shared = jnp.where(low_lanes, top[:, PADDED - LANES :], bottom[:, :LANES])
        return jnp.concatenate([top[:, : PADDED - LANES], shared, bottom[:, LANES:]], axis=1)

    for step in FAR_FIRST:
        target = (z + step) % N
        term_send[target] = second_term(target).astype(jnp.bfloat16)
        term_copy(target, z).start()
    second_total = second_term(z)
    w_pass_on(4)
    x_receive(1)
    x_send(2)

    for source in range(N):
        wc_copy(source, 1 - core).wait_recv()
    order = (0,) + NEAR_FIRST
    for pair in range(HALF):
        sources = [(y + step) % N for step in order[2 * pair : 2 * pair + 2]]
        for step, source in zip(order[2 * pair : 2 * pair + 2], sources):
            if step:
                gather_copy(source, source).wait_recv()
        product = lax.dot_general(
            jnp.concatenate([weights[source] for source in sources], axis=1),
            jnp.concatenate([gathered[source] for source in sources], axis=1),
            (((1,), (1,)), ((), ())),
            preferred_element_type=jnp.float32,
        )
        if pair == 0:
            unit_total[...] = product
        elif pair < HALF - 1:
            unit_total[...] += product
        else:
            unit_send[...] = (unit_total[...] + product).astype(jnp.bfloat16).reshape(N, UNITS, MERGED)

    def unit_copy(target, source):
        return remote(
            unit_send.at[target], unit_recv.at[source], unit_s.at[target], unit_r.at[source], at_x(target)
        )

    for step in FAR_FIRST:
        unit_copy((x + step) % N, x).start()
    x_receive(2)
    x_send(3)
    units = unit_send[x].astype(jnp.float32)
    for step in NEAR_FIRST:
        source = (x + step) % N
        unit_copy(source, source).wait_recv()
        units = units + unit_recv[source].astype(jnp.float32)
    grads = (units * slope).astype(jnp.bfloat16)
    pres[core, z] = grads
    pre_ref[...] = grads

    def pre_copy(target, source):
        return remote(
            pres.at[core, source], pres.at[core, source], pre_s.at[target], pre_r.at[source], at_z(target)
        )

    def pt_copy(source, owner):
        return remote(pres.at[owner, source], pres.at[owner, source], pt_s.at[source], pt_r.at[source], twin)

    for step in FAR_FIRST:
        pre_copy((z + step) % N, z).start()
    pt_copy(z, core).start()

    for step in NEAR_FIRST:
        source = (z + step) % N
        term_copy(source, source).wait_recv()
        second_total = second_total + term_recv[source].astype(jnp.float32)
    second_total = second_total * factor
    second_ref[:, : LANES // 2] = second_total[:, :PADDED].T[:OWN]
    second_ref[:, LANES // 2 :] = pltpu.roll(second_total[:, PAIR - PADDED :], OWN, 1).T[:OWN]

    for step in NEAR_FIRST:
        source = (z + step) % N
        pre_copy(source, source).wait_recv()
        pt_copy(source, core).start()
    x_receive(3)
    for source in range(N):
        pt_copy(source, 1 - core).wait_recv()
    depth = N * MERGED
    low = jnp.dot(
        jnp.concatenate([pres[0, k] for k in range(N)], axis=1),
        inputs[:, :, :PADDED].reshape(depth, PADDED),
        preferred_element_type=jnp.float32,
    )
    high = jnp.dot(
        jnp.concatenate([pres[1, k] for k in range(N)], axis=1),
        inputs[:, :, PAIR - PADDED :].reshape(depth, PADDED),
        preferred_element_type=jnp.float32,
    )
    first_ref[...] = ((low + pltpu.roll(high, OWN, 1)) * factor)[:, :OWN]

    for step in range(1, N):
        ya_copy((y + step) % N, y).wait_send()
        yb_copy((y + step) % N, y).wait_send()
        xa_copy((x + step) % N, x).wait_send()
        xb_copy((x + step) % N, x).wait_send()
        gather_copy((y + step) % N, y).wait_send()
        unit_copy((x + step) % N, x).wait_send()
        term_copy((z + step) % N, z).wait_send()
        pre_copy((z + step) % N, z).wait_send()
        pz_copy((z + step) % N, z).wait_send()
    w_finish()
    x_finish()
    for source in range(N):
        wc_copy(source, core).wait_send()
        pt_copy(source, core).wait_send()

    @pl.when(sender)
    def _():
        for step in range(1, N):
            wy_copy((y + step) % N, y).wait_send()

    for copy in (swap_inputs, swap_hidden, swap_merged):
        copy.wait_send()


def body(row_grads, row_dest, merger_in, hidden_pre, w_second):
    factor = 1.0 / math.sqrt(merger_in.shape[1] * lax.axis_size("enc"))
    width = merger_in.shape[2]
    bf16 = jnp.bfloat16
    vmem = pl.BlockSpec(memory_space=pltpu.VMEM)
    hbm = pl.BlockSpec(memory_space=pltpu.HBM)
    sems = pltpu.SemaphoreType.DMA
    pre, first, second = pl.pallas_call(
        functools.partial(kernel, factor),
        out_shape=(
            jax.ShapeDtypeStruct((UNITS, MERGED), bf16),
            jax.ShapeDtypeStruct((UNITS, OWN), jnp.float32),
            jax.ShapeDtypeStruct((OWN, LANES), jnp.float32),
        ),
        in_specs=[hbm, vmem, hbm, hbm, hbm],
        out_specs=(vmem, vmem, vmem),
        scratch_shapes=[
            pltpu.VMEM((SLOTS, N * N * LANES), bf16),
            pltpu.VMEM((SHARE, width), bf16),
            pltpu.VMEM((MERGED, width), bf16),
            pltpu.VMEM((N, N, ROWS, LANES), bf16),
            pltpu.VMEM((N, N, ROWS, LANES), bf16),
            pltpu.VMEM((N, PROMPTS, ROWS, LANES), bf16),
            pltpu.VMEM((N, PROMPTS, ROWS, LANES), bf16),
            pltpu.VMEM((N, ROWS, LANES), bf16),
            pltpu.VMEM((N, ROWS, LANES), bf16),
            pltpu.VMEM((N, ROWS, N * LANES), bf16),
            pltpu.VMEM((N, ROWS, N * LANES), bf16),
            pltpu.VMEM((N, MERGED, LANES), bf16),
            pltpu.VMEM((MERGED, LANES), bf16),
            pltpu.VMEM((N, PAIR, LANES), bf16),
            pltpu.VMEM((2, N, MERGED, PADDED), bf16),
            pltpu.VMEM((N, MERGED, PADDED), bf16),
            pltpu.VMEM((N, SHARE, PAIR), bf16),
            pltpu.VMEM((N, SHARE, PAIR), bf16),
            pltpu.VMEM((N, SHARE, PAIR), bf16),
            pltpu.VMEM((N, SHARE, PAIR), bf16),
            pltpu.VMEM((N, MERGED, PAIR), bf16),
            pltpu.VMEM((N, LANES // 2, PAIR), bf16),
            pltpu.VMEM((N, LANES // 2, PAIR), bf16),
            pltpu.VMEM((PAIR, MERGED), jnp.float32),
            pltpu.VMEM((N, UNITS, MERGED), bf16),
            pltpu.VMEM((N, UNITS, MERGED), bf16),
            pltpu.VMEM((2, N, UNITS, MERGED), bf16),
            sems((4,)),
        ]
        + [sems((N,)) for _ in range(12)]
        + [sems((HALF,)) for _ in range(4)]
        + [sems((N,)) for _ in range(4)]
        + [sems((HALF,)) for _ in range(4)]
        + [sems((N,)) for _ in range(8)]
        + [sems((3,)), sems((3,))],
        compiler_params=pltpu.CompilerParams(
            collective_id=0, has_side_effects=True, vmem_limit_bytes=54700 * 1024
        ),
    )(row_grads, row_dest, merger_in, hidden_pre, w_second)
    return pre.T[None], first.T, second


def solution(mesh):
    return jax.shard_map(
        body,
        mesh=mesh,
        in_specs=(
            P("enc", "roll", None),
            P("enc", "roll"),
            P("enc", None, None),
            P("enc", None, None),
            P(None, "roll"),
        ),
        out_specs=(P("enc", None, "roll"), P("enc", "roll"), P("enc", "roll")),
        check_vma=False,
    )
```

time: 77.7 us -> 72.6 us (0.934)
  Pallas kernels: 72.3 us -> 69.2 us
  local copies, waits for them, and re-layouts: 4.48 us -> 2.57 us
    pallas_call x1, Pallas kernels: 72.3 us -> 69.2 us  [body(): pl.pallas_call(functools.partial(kernel, factor), out_shape=(jax.ShapeDty...]
    unnamed x3 -> x5, local copies, waits for them, and re-layouts: 4.48 us -> 2.57 us
where the time goes in v3:
time: 72.6 us; the launch traced here: 72.4 us
  Pallas kernels  69.2 us (95%)
  local copies, waits for them, and re-layouts  2.57 us (4%)
    pallas_call x1, Pallas kernels, body(): pl.pallas_call(functools.partial(kernel, factor), out_shape=(jax.ShapeDty...  69.2 us
    unnamed x5, local copies, waits for them, and re-layouts  2.57 us

profile of v3, /device:TPU:1, one launch (start us, length us, event | category | flops | bytes accessed | tf_op | source)
XLA Modules:
  0.0 72.4 jit_solution(3194761906491177367)
XLA Ops:
  0.6 0.0 copy-start
  0.6 0.6 copy-done
  1.3 69.2 %shard_map.76 = (bf16[80,128]{1,0:T(8,128)(2,1)S(1)}, f32[80,320]{1,0:T(8,128)S(1)}, f32[320,128]{1,0:T(8,128)S(1)}) custom-call(bf16[1,32,8192]{2,1,0:T(8,128)(2,1)} %rows_hbm.1, s32[1,32]{1,0:T(1,128)S(1)} %copy-done, bf16[1,128,5120]{2,1,0:T(8,128)(2,1)} %merger_hbm.1, bf16[1,128,5120]{2,1,0:T(8,128)(2,1)} %before_hbm.1, bf16[5120,128]{1,0:T(8,128)(2,1)} %w_hbm.1), custom_call_target="tpu_custom_call" | custom-call | tf_op jit(solution)/shard_map/pallas_call | solution.py:439
  70.5 0.6 copy.11
  71.1 0.6 copy.12
  71.7 0.7 copy.13
Async XLA Ops:
  0.6 0.7 copy-start

commit v4 on v3

--- a/solution.py
+++ b/solution.py
@@ -45,7 +45,7 @@
     weights, hidden, other_hidden, pack_own, pack_swap, pack_other, pack_send, inputs, term_send, term_recv,
     unit_total, unit_send, unit_recv, pres,
     local_sem, ya_s, ya_r, yb_s, yb_r, xa_s, xa_r, xb_s, xb_r, gather_s, gather_r, wy_s, wy_r,
-    wu_s, wu_r, wd_s, wd_r, wc_s, wc_r, pz_s, pz_r, xu_s, xu_r, xd_s, xd_r,
+    wz_s, wz_r, wc_s, wc_r, pz_s, pz_r, xu_s, xu_r, xd_s, xd_r,
     unit_s, unit_r, term_s, term_r, pre_s, pre_r, pt_s, pt_r, core_s, core_r,
 ):
     enc = lax.axis_index("enc")
@@ -111,6 +111,32 @@
     load_before = pltpu.make_async_copy(before_hbm.at[0], before, local_sem.at[2])
     load_merger.start()
     load_before.start()
+
+    pl.semaphore_wait(barrier, 3 * (N - 1) + 1)
+
+    sender = y // HALF == core
+
+    def w_block(zz, owner):
+        return weights.at[pl.ds(owner * HALF, HALF), pl.ds(pl.multiple_of(zz * UNITS, 16), UNITS), :]
+
+    def wy_copy(target, source):
+        return remote(
+            w_hbm.at[pl.ds(pl.multiple_of(z * PAIR + target * UNITS, 16), UNITS), :],
+            weights.at[source, pl.ds(pl.multiple_of(z * UNITS, 16), UNITS), :],
+            wy_s.at[target], wy_r.at[source], at_y(target),
+        )
+
+    own_w = pltpu.make_async_copy(
+        w_hbm.at[pl.ds(pl.multiple_of(z * PAIR + y * UNITS, 16), UNITS), :],
+        weights.at[y, pl.ds(pl.multiple_of(z * UNITS, 16), UNITS), :],
+        local_sem.at[3],
+    )
+
+    @pl.when(sender)
+    def _():
+        own_w.start()
+        for step in FAR_FIRST:
+            wy_copy((y + step) % N, y).start()
 
     load_rows.wait()
     base = (x // PROMPT_X) * SLOTS
@@ -124,41 +150,46 @@
         for part in range(N):
             ya_send[part, block] = placed[:ROWS, part * LANES : (part + 1) * LANES]
 
-    pl.semaphore_wait(barrier, 3 * (N - 1) + 1)
-
-    sender = y // HALF == core
-
-    def w_block(zz, owner):
-        return weights.at[pl.ds(owner * HALF, HALF), pl.ds(pl.multiple_of(zz * UNITS, 16), UNITS), :]
-
-    def wy_copy(target, source):
-        return remote(
-            w_hbm.at[pl.ds(pl.multiple_of(z * PAIR + target * UNITS, 16), UNITS), :],
-            weights.at[source, pl.ds(pl.multiple_of(z * UNITS, 16), UNITS), :],
-            wy_s.at[target], wy_r.at[source], at_y(target),
-        )
-
-    own_w = pltpu.make_async_copy(
-        w_hbm.at[pl.ds(pl.multiple_of(z * PAIR + y * UNITS, 16), UNITS), :],
-        weights.at[y, pl.ds(pl.multiple_of(z * UNITS, 16), UNITS), :],
-        local_sem.at[3],
-    )
+    def ya_copy(target, source):
+        return remote(ya_send.at[target], ya_recv.at[source], ya_s.at[target], ya_r.at[source], at_y(target))
+
+    def xb_copy(target, source):
+        return remote(xb_send.at[target], xb_recv.at[source], xb_s.at[target], xb_r.at[source], at_x(target))
+
+    for step in FAR_FIRST:
+        ya_copy((y + step) % N, y).start()
+        xb_copy((x + step) % N, x).start()
 
     @pl.when(sender)
     def _():
-        own_w.start()
-        for step in FAR_FIRST:
-            wy_copy((y + step) % N, y).start()
-
-    def ya_copy(target, source):
-        return remote(ya_send.at[target], ya_recv.at[source], ya_s.at[target], ya_r.at[source], at_y(target))
-
-    def xb_copy(target, source):
-        return remote(xb_send.at[target], xb_recv.at[source], xb_s.at[target], xb_r.at[source], at_x(target))
-
-    for step in FAR_FIRST:
-        ya_copy((y + step) % N, y).start()
-        xb_copy((x + step) % N, x).start()
+        own_w.wait()
+
+    for step in range(HALF):
+        source = core * HALF + step
+
+        @pl.when(source != y)
+        def _():
+            wy_copy(source, source).wait_recv()
+
+    first_hop = ((2, 0), (N - 2, 1), (1, 2), (N - 1, 3))
+    second_hop = ((N - 2, 1, 4), (N - 2, 2, 5), (2, N - 1, 6))
+
+    def wz_copy(source, target, send):
+        block = w_block(source, core)
+        return remote(block, block, wz_s.at[send], wz_r.at[source], at_z(target))
+
+    def w_arrived(distances):
+        for distance in distances:
+            source = (z + distance) % N
+            wz_copy(source, source, 0).wait_recv()
+            wc_copy(source, core).start()
+
+    def wc_copy(source, owner):
+        return remote(w_block(source, owner), w_block(source, owner), wc_s.at[source], wc_r.at[source], twin)
+
+    for distance, send in first_hop:
+        wz_copy(z, (z + distance) % N, send).start()
+    wc_copy(z, core).start()
 
     load_merger.wait()
     for block in range(N):
@@ -177,32 +208,9 @@
         hidden[1, block] = pltpu.roll(value, OWN, 1)[:, :PADDED].astype(jnp.bfloat16)
         return carry
 
-    lax.fori_loop(0, HALF, activate, 0)
-
-    @pl.when(sender)
-    def _():
-        own_w.wait()
-
-    for step in range(HALF):
-        source = core * HALF + step
-
-        @pl.when(source != y)
-        def _():
-            wy_copy(source, source).wait_recv()
-
-    w_send, w_receive, w_finish = ring(lambda zz: w_block(zz, core), z, at_z, wu_s, wu_r, wd_s, wd_r)
-
-    def wc_copy(source, owner):
-        return remote(w_block(source, owner), w_block(source, owner), wc_s.at[source], wc_r.at[source], twin)
-
-    def w_pass_on(step):
-        for source in w_receive(step - 1):
-            wc_copy(source, core).start()
-        if step < HALF:
-            w_send(step)
-
-    w_send(0)
-    wc_copy(z, core).start()
+    lax.fori_loop(0, N, activate, 0)
+    swap_hidden = remote(hidden.at[1 - core], other_hidden, core_s.at[1], core_r.at[1], twin)
+    swap_hidden.start()
 
     swap_inputs.wait_recv()
     lane_core = lax.broadcasted_iota(jnp.int32, (SHARE, PAIR), 1) // OWN
@@ -223,11 +231,6 @@
         lambda owner: inputs.at[:, pl.ds(pl.multiple_of(owner * SHARE, SHARE), SHARE), :],
         x, at_x, xu_s, xu_r, xd_s, xd_r,
     )
-
-    lax.fori_loop(HALF, N, activate, 0)
-    swap_hidden = remote(hidden.at[1 - core], other_hidden, core_s.at[1], core_r.at[1], twin)
-    swap_hidden.start()
-    w_pass_on(1)
 
     limit = before.shape[1] - 2 * LANES
     first = jnp.minimum((roll * UNITS) // LANES * LANES, limit)
@@ -240,6 +243,11 @@
     own_before = lax.dot_general(select, window, (((1,), (1,)), ((), ())), preferred_element_type=jnp.float32)
     slope = gelu_slope(own_before)
 
+    w_arrived((2, N - 2))
+    for origin, distance, send in second_hop:
+        wz_copy((z + origin) % N, (z + distance) % N, send).start()
+    w_arrived((1, N - 1))
+
     def yb_copy(target, source):
         return remote(yb_send.at[target], yb_recv.at[source], yb_s.at[target], yb_r.at[source], at_y(target))
 
@@ -270,7 +278,6 @@
         source = (z + step) % N
         pz_copy(source, source).wait_recv()
     x_send(0)
-    w_pass_on(2)
 
     lower = yb_send[y].astype(jnp.float32)
     for step in NEAR_FIRST:
@@ -292,9 +299,6 @@
         gather_copy((y + step) % N, y).start()
     swap_merged = remote(gathered.at[y], other_merged, core_s.at[2], core_r.at[2], twin)
     swap_merged.start()
-    w_pass_on(3)
-    x_receive(0)
-    x_send(1)
 
     def term_copy(target, source):
         return remote(term_send.at[target], term_recv.at[source], term_s.at[target], term_r.at[source], at_z(target))
@@ -320,10 +324,11 @@
         target = (z + step) % N
         term_send[target] = second_term(target).astype(jnp.bfloat16)
         term_copy(target, z).start()
+        if step == FAR_FIRST[HALF]:
+            w_arrived((3, N - 3, HALF))
+    x_receive(0)
+    x_send(1)
     second_total = second_term(z)
-    w_pass_on(4)
-    x_receive(1)
-    x_send(2)
 
     for source in range(N):
         wc_copy(source, 1 - core).wait_recv()
@@ -353,8 +358,8 @@
 
     for step in FAR_FIRST:
         unit_copy((x + step) % N, x).start()
-    x_receive(2)
-    x_send(3)
+    x_receive(1)
+    x_send(2)
     units = unit_send[x].astype(jnp.float32)
     for step in NEAR_FIRST:
         source = (x + step) % N
@@ -375,6 +380,8 @@
     for step in FAR_FIRST:
         pre_copy((z + step) % N, z).start()
     pt_copy(z, core).start()
+    x_receive(2)
+    x_send(3)
 
     for step in NEAR_FIRST:
         source = (z + step) % N
@@ -414,7 +421,10 @@
         term_copy((z + step) % N, z).wait_send()
         pre_copy((z + step) % N, z).wait_send()
         pz_copy((z + step) % N, z).wait_send()
-    w_finish()
+    for distance, send in first_hop:
+        wz_copy(z, (z + distance) % N, send).wait_send()
+    for origin, distance, send in second_hop:
+        wz_copy((z + origin) % N, (z + distance) % N, send).wait_send()
     x_finish()
     for source in range(N):
         wc_copy(source, core).wait_send()
@@ -475,9 +485,7 @@
             pltpu.VMEM((2, N, UNITS, MERGED), bf16),
             sems((4,)),
         ]
-        + [sems((N,)) for _ in range(12)]
-        + [sems((HALF,)) for _ in range(4)]
-        + [sems((N,)) for _ in range(4)]
+        + [sems((N,)) for _ in range(18)]
         + [sems((HALF,)) for _ in range(4)]
         + [sems((N,)) for _ in range(8)]
         + [sems((3,)), sems((3,))],

time: 72.6 us -> 72.1 us (level)
  no operation moved by 1% of the time
where the time goes in v4:
time: 72.1 us; the launch traced here: 71.8 us
  Pallas kernels  68.6 us (95%)
  local copies, waits for them, and re-layouts  2.57 us (4%)
    pallas_call x1, Pallas kernels, body(): pl.pallas_call(functools.partial(kernel, factor), out_shape=(jax.ShapeDty...  68.6 us
    unnamed x5, local copies, waits for them, and re-layouts  2.57 us

profile of v4, /device:TPU:1, one launch (start us, length us, event | category | flops | bytes accessed | tf_op | source)
XLA Modules:
  0.0 71.8 jit_solution(5931841658294189449)
XLA Ops:
  0.6 0.0 copy-start
  0.6 0.6 copy-done
  1.3 68.6 %shard_map.76 = (bf16[80,128]{1,0:T(8,128)(2,1)S(1)}, f32[80,320]{1,0:T(8,128)S(1)}, f32[320,128]{1,0:T(8,128)S(1)}) custom-call(bf16[1,32,8192]{2,1,0:T(8,128)(2,1)} %rows_hbm.1, s32[1,32]{1,0:T(1,128)S(1)} %copy-done, bf16[1,128,5120]{2,1,0:T(8,128)(2,1)} %merger_hbm.1, bf16[1,128,5120]{2,1,0:T(8,128)(2,1)} %before_hbm.1, bf16[5120,128]{1,0:T(8,128)(2,1)} %w_hbm.1), custom_call_target="tpu_custom_call" | custom-call | tf_op jit(solution)/shard_map/pallas_call | solution.py:449
  69.9 0.6 copy.11
  70.5 0.6 copy.12
  71.2 0.7 copy.13
Async XLA Ops:
  0.6 0.7 copy-start
